TPU v7x, 32 devices: a whole 2x2x4 slice. The times are simulated.
32 devices in a mesh: rot: 4 (over y, x), space: 8 (over z, core).
Axes of the slice: x: 2, y: 2, z: 4, core: 2. Of those that a mesh axis runs over, the one named last changes fastest.
Arguments:
- raster: bfloat16 [4, 128, 2, 256], P(None, 'space'), may hold values from -6 to 6
- coarse_features: bfloat16 [4, 64, 128, 2, 256], P('rot', None, 'space'), may hold values from -6 to 6
- lift_weight: bfloat16 [4, 9, 64, 4], P('rot'), may hold values from -1 to 1
- lift_bias: float32 [64], replicated, may hold values from -3 to 3
- group_weight: bfloat16 [4, 9, 64, 64], P('rot'), may hold values from -0.125 to 0.125
- group_bias: float32 [64], replicated, may hold values from -3 to 3
Outputs:
- features: bfloat16 [4, 64, 128, 2, 256], P('rot', None, 'space')
All inputs are finite; a program needn't handle non-finite values.
Results may differ from a plain program's by a relative error of at most 0.0045.
Values may be sent and summed in bfloat16 or wider, within the bound.
A program may use at most 192 MiB of HBM per device.

v0:
```python
import functools

import jax
import jax.numpy as jnp
from jax import lax
from jax.experimental import pallas as pl
from jax.experimental.pallas import tpu as pltpu
from jax.sharding import PartitionSpec as P

MESH = pl.DeviceIdType.MESH
STEP = 2


def send_order(chunks):
    return [1, 2, 0, chunks - 1, chunks - 2] + list(range(3, chunks - 2))


def mix_order(chunks):
    got, done, plan = set(), set(), []
    for place, j in enumerate(send_order(chunks)):
        got.add(j)
        ready = [
            i
            for i in range(1, chunks - 1)
            if i not in done and {i - 1, i, i + 1} <= got
        ]
        done.update(ready)
        if place == 4:
            ready.append(0)
        if place == 5:
            ready.append(chunks - 1)
        plan.append((j, ready))
    return plan


def column(row):
    n = row.shape[1]
    shape = (n, n)
    same = lax.broadcasted_iota(jnp.int32, shape, 0) == lax.broadcasted_iota(jnp.int32, shape, 1)
    return jnp.sum(jnp.where(same, row, 0.0), axis=1, keepdims=True)


def packed_filter(weight_ref):
    w = [weight_ref[i] for i in range(9)]
    half = w[0].shape[0] // 2
    parts = [jnp.concatenate([w[dx], w[3 + dx]], 1) for dx in range(3)]
    late = jnp.concatenate(w[6:], 0)
    parts.append(jnp.concatenate([late[: 3 * half], late[3 * half :]], 1))
    return jnp.concatenate(parts, 0)


def opened_filter(packed):
    lanes = packed.shape[1] // 2
    top = packed[: 6 * lanes // 2]
    late = packed[6 * lanes // 2 :]
    return jnp.concatenate([top, jnp.concatenate([late[:, :lanes], late[:, lanes:]], 0)], 1)


def kernel(
    rots,
    spaces,
    cin,
    coarse_ref,
    raster_ref,
    lift_ref,
    lift_bias_hbm,
    filter_hbm,
    group_bias_hbm,
    out_ref,
    lift_bias_ref,
    filter_ref,
    group_bias_ref,
    load_s,
    hid,
    rext,
    packed,
    filters,
    stacked,
    acc,
    part_out,
    part_in,
    hid_s,
    hid_r,
    up_s,
    up_r,
    down_s,
    down_r,
    ras_s,
    ras_r,
    fil_s,
    fil_r,
    mate_s,
    mate_r,
    par_s,
    par_r,
):
    g = lax.axis_index("rot")
    s = lax.axis_index("space")
    half = rots // 2
    tiles, rows, ch, cols = coarse_ref.shape
    chunks = rows // STEP
    hi, lo = g // half, lax.rem(g, half)

    def low(k):
        return hi * half + lax.rem(lo + k, half)

    def high(k):
        return lax.rem(g + k * half, rots)

    def gather_group(t):
        return (low, half) if t % 2 == 0 else (high, 2)

    def sum_group(t):
        return (high, 2) if t % 2 == 0 else (low, half)

    has_up = s > 0
    has_down = s < spaces - 1

    def hidden_copy(t, k, j):
        member, n = gather_group(t)
        span = pl.ds(1 + j * STEP, STEP)
        return pltpu.make_async_remote_copy(
            src_ref=hid.at[t, 0, span],
            dst_ref=hid.at[t, n - k, span],
            send_sem=hid_s.at[t, k - 1, j],
            recv_sem=hid_r.at[t, n - k - 1, j],
            device_id=(member(k), s),
            device_id_type=MESH,
        )

    def up_copy(t, k):
        return pltpu.make_async_remote_copy(
            src_ref=hid.at[t, k, 1],
            dst_ref=hid.at[t, k, rows + 1],
            send_sem=up_s.at[t, k],
            recv_sem=up_r.at[t, k],
            device_id=(g, s - 1),
            device_id_type=MESH,
        )

    def down_copy(t, k):
        return pltpu.make_async_remote_copy(
            src_ref=hid.at[t, k, rows],
            dst_ref=hid.at[t, k, 0],
            send_sem=down_s.at[t, k],
            recv_sem=down_r.at[t, k],
            device_id=(g, s + 1),
            device_id_type=MESH,
        )

    def raster_copy(way):
        src, dst, to = ((1, rows + 1, s - 1), (rows, 0, s + 1))[way]
        return pltpu.make_async_remote_copy(
            src_ref=rext.at[src],
            dst_ref=rext.at[dst],
            send_sem=ras_s.at[way],
            recv_sem=ras_r.at[way],
            device_id=(g, to),
            device_id_type=MESH,
        )

    side = lax.rem(s, 2)

    def filter_copy(k):
        return pltpu.make_async_remote_copy(
            src_ref=packed.at[0, side],
            dst_ref=packed.at[rots - k, side],
            send_sem=fil_s.at[k - 1],
            recv_sem=fil_r.at[rots - k - 1],
            device_id=(lax.rem(g + k, rots), s),
            device_id_type=MESH,
        )

    def mate_copy(k):
        return pltpu.make_async_remote_copy(
            src_ref=packed.at[k, side],
            dst_ref=packed.at[k, side],
            send_sem=mate_s.at[k - 1],
            recv_sem=mate_r.at[k - 1],
            device_id=(g, s + 1 - 2 * side),
            device_id_type=MESH,
        )

    def part_copy(t, k, j):
        member, n = sum_group(t)
        span = pl.ds(j * STEP, STEP)
        return pltpu.make_async_remote_copy(
            src_ref=part_out.at[t, k - 1, span],
            dst_ref=part_in.at[t, n - k - 1, span],
            send_sem=par_s.at[t, k - 1, j],
            recv_sem=par_r.at[t, n - k - 1, j],
            device_id=(member(k), s),
            device_id_type=MESH,
        )

    barrier = pltpu.get_barrier_semaphore()
    for k in range(1, rots):
        pl.semaphore_signal(barrier, inc=1, device_id=(lax.rem(g + k, rots), s), device_id_type=MESH)

    @pl.when(has_up)
    def _():
        pl.semaphore_signal(barrier, inc=1, device_id=(g, s - 1), device_id_type=MESH)

    @pl.when(has_down)
    def _():
        pl.semaphore_signal(barrier, inc=1, device_id=(g, s + 1), device_id_type=MESH)

    loads = [
        pltpu.make_async_copy(source, target, load_s.at[i])
        for i, (source, target) in enumerate(
            (
                (filter_hbm, filter_ref),
                (lift_bias_hbm, lift_bias_ref),
                (group_bias_hbm, group_bias_ref),
            )
        )
    ]
    for load in loads:
        load.start()

    pixel = lax.broadcasted_iota(jnp.int32, raster_ref.shape[1:], 1)
    wide = tiles * cols

    def spread_row(r, carry):
        mid = raster_ref[r].astype(jnp.float32)
        left = jnp.where(pixel % cols == 0, 0.0, pltpu.roll(mid, 1, 1))
        right = jnp.where(pixel % cols == cols - 1, 0.0, pltpu.roll(mid, wide - 1, 1))
        taps = left + pltpu.roll(mid, cin, 0) + pltpu.roll(right, 2 * cin, 0)
        rext[r + 1] = taps.astype(rext.dtype)
        return carry

    lax.fori_loop(0, rows, spread_row, 0, unroll=True)
    for load in loads:
        load.wait()
    packed[0] = packed_filter(filter_ref).reshape(packed.shape[1:])
    zero_row = jnp.zeros((ch, cols), hid.dtype)

    @pl.when(jnp.logical_not(has_up))
    def _():
        rext[0] = jnp.zeros(rext.shape[1:], rext.dtype)
        for t in range(tiles):
            for k in range(gather_group(t)[1]):
                hid[t, k, 0] = zero_row

    @pl.when(jnp.logical_not(has_down))
    def _():
        rext[rows + 1] = jnp.zeros(rext.shape[1:], rext.dtype)
        for t in range(tiles):
            for k in range(gather_group(t)[1]):
                hid[t, k, rows + 1] = zero_row

    around = has_up.astype(jnp.int32) + has_down.astype(jnp.int32)
    pl.semaphore_wait(barrier, rots - 1 + around)

    @pl.when(has_up)
    def _():
        raster_copy(0).start()

    @pl.when(has_down)
    def _():
        raster_copy(1).start()

    for k in range(1, rots):
        filter_copy(k).start()

    lift_bias = column(lift_bias_ref[...])
    group_bias = column(group_bias_ref[...])

    def lift_row(r, carry):
        taps = rext[pl.ds(r, 3)].reshape(3 * rext.shape[1], rext.shape[2])
        lifted = jnp.dot(lift_ref[...], taps, preferred_element_type=jnp.float32)
        for t in range(tiles):
            total = lifted[:, t * cols : (t + 1) * cols] + lift_bias
            total = total + coarse_ref[t, r].astype(jnp.float32)
            hid[t, 0, r + 1] = jnp.maximum(total, 0.0).astype(hid.dtype)
        return carry

    for place, j in enumerate(send_order(chunks)):
        if place == 2:

            @pl.when(has_down)
            def _():
                raster_copy(0).wait_recv()

            @pl.when(has_up)
            def _():
                raster_copy(1).wait_recv()

        lax.fori_loop(j * STEP, (j + 1) * STEP, lift_row, 0, unroll=True)
        for t in range(tiles):
            for k in range(1, gather_group(t)[1]):
                hidden_copy(t, k, j).start()
        if j == 0:

            @pl.when(has_up)
            def _():
                for t in range(tiles):
                    up_copy(t, 0).start()

        if j == chunks - 1:

            @pl.when(has_down)
            def _():
                for t in range(tiles):
                    down_copy(t, 0).start()

    for k in range(1, rots):
        filter_copy(k).wait_recv()
        mate_copy(rots - k).start()
    filters[0] = opened_filter(packed[0].reshape(-1, packed.shape[3]))
    for k in range(1, rots):
        mate_copy(k).wait_recv()
        filters[k] = opened_filter(packed[k].reshape(-1, packed.shape[3]))
    height = filters.shape[1]
    for t in range(tiles):
        take, n_take = gather_group(t)
        give, n_give = sum_group(t)
        for h in range(n_take):
            for p in range(n_give):
                relative = lax.rem(give(p) - take(h) + rots, rots)
                place = lax.rem(relative - g + rots, rots)
                stacked[t, h, p * height : (p + 1) * height] = filters[place]

    lane = lax.broadcasted_iota(jnp.int32, (ch, cols), 1)

    def mix(t, j):
        n_take = gather_group(t)[1]
        n_give = sum_group(t)[1]

        def one_row(r, carry):
            total = None
            for h in range(n_take):
                rim = hid[t, h, pl.ds(r, 3)].reshape(3 * ch, cols)
                term = jnp.dot(
                    stacked[t, h, : n_give * height], rim, preferred_element_type=jnp.float32
                )
                total = term if total is None else total + term
            for p in range(n_give):
                left = total[p * height : p * height + ch]
                mid = total[p * height + ch : p * height + 2 * ch]
                right = total[p * height + 2 * ch : (p + 1) * height]
                left = jnp.where(lane == 0, 0.0, pltpu.roll(left, 1, 1))
                right = jnp.where(lane == cols - 1, 0.0, pltpu.roll(right, cols - 1, 1))
                value = mid + left + right
                if p == 0:
                    acc[t, r] = value + group_bias
                else:
                    part_out[t, p - 1, r] = value.astype(part_out.dtype)
            return carry

        lax.fori_loop(j * STEP, (j + 1) * STEP, one_row, 0, unroll=True)
        for k in range(1, n_give):
            part_copy(t, k, j).start()

    finished = []
    for j, ready in mix_order(chunks):
        for t in range(tiles):
            n_take = gather_group(t)[1]
            for k in range(1, n_take):
                hidden_copy(t, k, j).wait_recv()
            if j == 0:

                @pl.when(has_up)
                def _():
                    for k in range(1, n_take):
                        up_copy(t, k).start()

            if j == chunks - 1:

                @pl.when(has_down)
                def _():
                    for k in range(1, n_take):
                        down_copy(t, k).start()

        for i in ready:
            for t in range(tiles):
                n_take = gather_group(t)[1]
                if i == 0:

                    @pl.when(has_up)
                    def _():
                        for k in range(n_take):
                            down_copy(t, k).wait_recv()

                if i == chunks - 1:

                    @pl.when(has_down)
                    def _():
                        for k in range(n_take):
                            up_copy(t, k).wait_recv()

                mix(t, i)
            finished.append(i)

    for j in finished:
        for t in range(tiles):
            n_give = sum_group(t)[1]
            for k in range(1, n_give):
                part_copy(t, k, j).wait_recv()

        for r in range(j * STEP, (j + 1) * STEP):
            totals = []
            for t in range(tiles):
                total = acc[t, r]
                for k in range(1, sum_group(t)[1]):
                    total = total + part_in[t, k - 1, r].astype(jnp.float32)
                totals.append(jnp.maximum(total, 0.0))
            out_ref[:, r] = jnp.stack(totals, 1).astype(out_ref.dtype)

    for k in range(1, rots):
        filter_copy(k).wait_send()
        mate_copy(k).wait_send()
    for t in range(tiles):
        for j in range(chunks):
            for k in range(1, gather_group(t)[1]):
                hidden_copy(t, k, j).wait_send()
            for k in range(1, sum_group(t)[1]):
                part_copy(t, k, j).wait_send()

    @pl.when(has_up)
    def _():
        raster_copy(0).wait_send()
        for t in range(tiles):
            for k in range(gather_group(t)[1]):
                up_copy(t, k).wait_send()

    @pl.when(has_down)
    def _():
        raster_copy(1).wait_send()
        for t in range(tiles):
            for k in range(gather_group(t)[1]):
                down_copy(t, k).wait_send()


def shards(rots, spaces, raster, coarse, lift_weight, lift_bias, group_weight, group_bias):
    ch, cin = lift_weight.shape[2:]
    _, rows, tiles, cols = raster.shape
    half = rots // 2
    most = max(half, 2)
    coarse_in = jnp.transpose(coarse[0], (2, 1, 0, 3))
    depth = -(-3 * cin // 16) * 16
    taps = jnp.transpose(raster, (1, 0, 2, 3)).reshape(rows, cin, tiles * cols)
    taps = jnp.pad(taps, ((0, 0), (0, depth - cin), (0, 0)))
    lift = jnp.transpose(lift_weight[0].reshape(3, 3, ch, cin), (2, 0, 1, 3)).reshape(ch, 3, 3 * cin)
    lift = jnp.pad(lift, ((0, 0), (0, 0), (0, depth - 3 * cin))).reshape(ch, 3 * depth)
    bf16, f32 = jnp.bfloat16, jnp.float32
    chunks = rows // STEP
    dma = pltpu.SemaphoreType.DMA
    out = pl.pallas_call(
        functools.partial(kernel, rots, spaces, cin),
        out_shape=jax.ShapeDtypeStruct((ch, rows, tiles, cols), bf16),
        in_specs=[pl.BlockSpec(memory_space=pltpu.VMEM)] * 3
        + [pl.BlockSpec(memory_space=pl.ANY)] * 3,
        out_specs=pl.BlockSpec(memory_space=pltpu.VMEM),
        scratch_shapes=[
            pltpu.VMEM((1, ch), f32),
            pltpu.VMEM((9, ch, ch), bf16),
            pltpu.VMEM((1, ch), f32),
            dma((3,)),
            pltpu.VMEM((tiles, most, rows + 2, ch, cols), bf16),
            pltpu.VMEM((rows + 2, depth, tiles * cols), bf16),
            pltpu.VMEM((rots, 2, 9 * ch // 4, 2 * ch), bf16),
            pltpu.VMEM((rots, 3 * ch, 3 * ch), bf16),
            pltpu.VMEM((tiles, most, most * 3 * ch, 3 * ch), bf16),
            pltpu.VMEM((tiles, rows, ch, cols), f32),
            pltpu.VMEM((tiles, most - 1, rows, ch, cols), bf16),
            pltpu.VMEM((tiles, most - 1, rows, ch, cols), bf16),
            dma((tiles, most - 1, chunks)),
            dma((tiles, most - 1, chunks)),
            dma((tiles, most)),
            dma((tiles, most)),
            dma((tiles, most)),
            dma((tiles, most)),
            dma((2,)),
            dma((2,)),
            dma((rots - 1,)),
            dma((rots - 1,)),
            dma((rots - 1,)),
            dma((rots - 1,)),
            dma((tiles, most - 1, chunks)),
            dma((tiles, most - 1, chunks)),
        ],
        compiler_params=pltpu.CompilerParams(
            collective_id=0, has_side_effects=True, vmem_limit_bytes=48 * 2**20
        ),
        name="mixing_layers",
    )(coarse_in, taps, lift, lift_bias[None], group_weight[0], group_bias[None])
    return out[None]


def solution(mesh):
    return jax.shard_map(
        functools.partial(shards, mesh.shape["rot"], mesh.shape["space"]),
        mesh=mesh,
        in_specs=(
            P(None, "space", None, None),
            P("rot", None, "space", None, None),
            P("rot", None, None, None),
            P(),
            P("rot", None, None, None),
            P(),
        ),
        out_specs=P("rot", None, "space", None, None),
        check_vma=False,
    )
```

profile of v0, /device:TPU:0, one launch (start us, length us, event | category | flops | bytes accessed | tf_op | source)
XLA Modules:
  0.0 35.3 jit_solution(16253130993589998130)
XLA Ops:
  0.0 0.0 copy-start.4
  0.0 0.0 copy-start.3
  0.0 0.7 %copy-done.4 = bf16[1,9,64,4]{2,3,1,0:T(4,128)(2,1)S(1)} copy-done((bf16[1,9,64,4]{2,3,1,0:T(4,128)(2,1)S(1)}, bf16[1,9,64,4]{2,3,1,0:T(4,128)(2,1)}, u32[]{:S(2)}) %copy-start.4) | copy-done | bytes 4632
  0.7 0.1 copy.12.lift_ref
  0.8 0.0 copy-done.3
  0.9 0.1 copy.13
  1.0 0.0 copy-start
  1.0 1.8 %copy.15 = bf16[1,64,16,2,256]{4,1,2,3,0:T(8,128)(2,1)S(1)} copy(bf16[1,64,16,2,256]{4,3,2,1,0:T(2,128)(2,1)} %param.7) | data formatting | bytes 2097152 | tf_op args[1]
  2.9 0.0 copy-start.1
  2.9 0.0 copy-start.2
  2.9 0.0 copy-done
  2.9 0.6 %copy-done.1 = f32[64]{0:T(128)S(1)} copy-done((f32[64]{0:T(128)S(1)}, f32[64]{0:T(128)}, u32[]{:S(2)}) %copy-start.1) | copy-done | bytes 280
  3.5 0.0 copy-done.2
  3.5 30.7 %mixing_layers.1 = bf16[64,16,2,256]{3,2,1,0:T(2,128)(2,1)S(1)} custom-call(bf16[2,16,64,256]{3,2,1,0:T(8,128)(2,1)S(1)} %bitcast.19, bf16[16,16,512]{2,1,0:T(8,128)(2,1)S(1)} %pad.8.raster_ref, bf16[64,48]{1,0:T(8,128)(2,1)S(1)} %copy.12.lift_ref, f32[1,64]{1,0:T(1,128)S(1)} %bitcast.21, bf16[9,64,64]{2,1,0:T(8,128)(2,1)S(1)} %bitcast.20, f32[1,64]{1,0:T(1,128)S(1)} %bitcast.22), custom_call_target="tpu_custom_call" | custom-call | tf_op jit(solution)/shard_map/mixing_layers/pallas_call | solution.py:449
  34.3 1.0 %copy.17 = bf16[1,64,16,2,256]{4,3,2,1,0:T(2,128)(2,1)} copy(bf16[1,64,16,2,256]{4,3,2,1,0:T(2,128)(2,1)S(1)} %bitcast.18) | data formatting | bytes 2097152
  (4 shorter events, 0.1 us)
Async XLA Ops:
  0.0 0.7 %copy-start.4 = (bf16[1,9,64,4]{2,3,1,0:T(4,128)(2,1)S(1)}, bf16[1,9,64,4]{2,3,1,0:T(4,128)(2,1)}, u32[]{:S(2)}) copy-start(bf16[1,9,64,4]{2,3,1,0:T(4,128)(2,1)} %param.8) | copy-start | bytes 13828
  0.0 0.9 %copy-start.3 = (bf16[4,16,2,256]{3,2,1,0:T(2,128)(2,1)S(1)}, bf16[4,16,2,256]{3,2,1,0:T(2,128)(2,1)}, u32[]{:S(2)}) copy-start(bf16[4,16,2,256]{3,2,1,0:T(2,128)(2,1)} %param.6) | copy-start | bytes 196612
  1.0 1.9 %copy-start = (bf16[1,9,64,64]{3,2,1,0:T(8,128)(2,1)S(1)}, bf16[1,9,64,64]{3,2,1,0:T(8,128)(2,1)}, u32[]{:S(2)}) copy-start(bf16[1,9,64,64]{3,2,1,0:T(8,128)(2,1)} %param.10) | copy-start | bytes 221188
  2.9 0.7 %copy-start.1 = (f32[64]{0:T(128)S(1)}, f32[64]{0:T(128)}, u32[]{:S(2)}) copy-start(f32[64]{0:T(128)} %param.9) | copy-start | bytes 772
  2.9 0.7 %copy-start.2 = (f32[64]{0:T(128)S(1)}, f32[64]{0:T(128)}, u32[]{:S(2)}) copy-start(f32[64]{0:T(128)} %param.11) | copy-start | bytes 772
where the time goes:
time: 35.5 us; the launch traced here: 35.3 us
  Pallas kernels  30.7 us (86%)
  local copies, waits for them, and re-layouts  4.45 us (13%)
    pallas_call x1, Pallas kernels, shards(): pl.pallas_call(functools.partial(kernel, rots, spaces, cin), out_shape=ja...  30.7 us
    unnamed x12, local copies, waits for them, and re-layouts  4.2 us

commit v1 on v0

--- a/solution.py
+++ b/solution.py
@@ -97,7 +97,7 @@
     g = lax.axis_index("rot")
     s = lax.axis_index("space")
     half = rots // 2
-    tiles, rows, ch, cols = coarse_ref.shape
+    ch, rows, tiles, cols = coarse_ref.shape
     chunks = rows // STEP
     hi, lo = g // half, lax.rem(g, half)
 
@@ -269,9 +269,10 @@
     def lift_row(r, carry):
         taps = rext[pl.ds(r, 3)].reshape(3 * rext.shape[1], rext.shape[2])
         lifted = jnp.dot(lift_ref[...], taps, preferred_element_type=jnp.float32)
+        both = coarse_ref[:, r].astype(jnp.float32)
         for t in range(tiles):
             total = lifted[:, t * cols : (t + 1) * cols] + lift_bias
-            total = total + coarse_ref[t, r].astype(jnp.float32)
+            total = total + both[:, t]
             hid[t, 0, r + 1] = jnp.maximum(total, 0.0).astype(hid.dtype)
         return carry
 
@@ -437,7 +438,6 @@
     _, rows, tiles, cols = raster.shape
     half = rots // 2
     most = max(half, 2)
-    coarse_in = jnp.transpose(coarse[0], (2, 1, 0, 3))
     depth = -(-3 * cin // 16) * 16
     taps = jnp.transpose(raster, (1, 0, 2, 3)).reshape(rows, cin, tiles * cols)
     taps = jnp.pad(taps, ((0, 0), (0, depth - cin), (0, 0)))
@@ -484,7 +484,7 @@
             collective_id=0, has_side_effects=True, vmem_limit_bytes=48 * 2**20
         ),
         name="mixing_layers",
-    )(coarse_in, taps, lift, lift_bias[None], group_weight[0], group_bias[None])
+    )(coarse[0], taps, lift, lift_bias[None], group_weight[0], group_bias[None])
     return out[None]
 
 

time: 35.5 us -> 35 us (0.986)
  local copies, waits for them, and re-layouts: 4.45 us -> 4.04 us
    unnamed x12 -> x13, local copies, waits for them, and re-layouts: 4.2 us -> 3.78 us
where the time goes in v1:
time: 35 us; the launch traced here: 34.8 us
  Pallas kernels  30.7 us (88%)
  local copies, waits for them, and re-layouts  4.04 us (12%)
    pallas_call x1, Pallas kernels, shards(): pl.pallas_call(functools.partial(kernel, rots, spaces, cin), out_shape=ja...  30.7 us
    unnamed x13, local copies, waits for them, and re-layouts  3.78 us

profile of v1, /device:TPU:0, one launch (start us, length us, event | category | flops | bytes accessed | tf_op | source)
XLA Modules:
  0.0 34.8 jit_solution(6301707968052256089)
XLA Ops:
  0.0 0.0 copy-start.5
  0.0 0.0 copy-start.4
  0.0 0.7 %copy-done.5 = bf16[1,9,64,4]{2,3,1,0:T(4,128)(2,1)S(1)} copy-done((bf16[1,9,64,4]{2,3,1,0:T(4,128)(2,1)S(1)}, bf16[1,9,64,4]{2,3,1,0:T(4,128)(2,1)}, u32[]{:S(2)}) %copy-start.5) | copy-done | bytes 4632
  0.7 0.1 copy.10.lift_ref
  0.8 0.0 copy-done.4
  0.9 0.1 copy.11
  1.0 0.0 copy-start.1
  1.0 0.0 copy-start.2
  1.0 0.0 copy-start.3
  1.0 0.8 %copy-done.1 = bf16[1,9,64,64]{3,2,1,0:T(8,128)(2,1)S(1)} copy-done((bf16[1,9,64,64]{3,2,1,0:T(8,128)(2,1)S(1)}, bf16[1,9,64,64]{3,2,1,0:T(8,128)(2,1)}, u32[]{:S(2)}) %copy-start.1) | copy-done | bytes 73752
  1.9 0.0 copy-done.2
  1.9 0.0 copy-done.3
  1.9 0.0 copy-start
  1.9 1.2 %copy-done = bf16[1,64,16,2,256]{4,3,2,1,0:T(2,128)(2,1)S(1)} copy-done((bf16[1,64,16,2,256]{4,3,2,1,0:T(2,128)(2,1)S(1)}, bf16[1,64,16,2,256]{4,3,2,1,0:T(2,128)(2,1)}, u32[]{:S(2)}) %copy-start) | copy-done | bytes 1048600
  3.1 30.7 %mixing_layers.1 = bf16[64,16,2,256]{3,2,1,0:T(2,128)(2,1)S(1)} custom-call(bf16[64,16,2,256]{3,2,1,0:T(2,128)(2,1)S(1)} %bitcast.15, bf16[16,16,512]{2,1,0:T(8,128)(2,1)S(1)} %pad.8.raster_ref, bf16[64,48]{1,0:T(8,128)(2,1)S(1)} %copy.10.lift_ref, f32[1,64]{1,0:T(1,128)S(1)} %bitcast.17, bf16[9,64,64]{2,1,0:T(8,128)(2,1)S(1)} %bitcast.16, f32[1,64]{1,0:T(1,128)S(1)} %bitcast.18), custom_call_target="tpu_custom_call" | custom-call | tf_op jit(solution)/shard_map/mixing_layers/pallas_call | solution.py:449
  33.9 1.0 %copy.13 = bf16[1,64,16,2,256]{4,3,2,1,0:T(2,128)(2,1)} copy(bf16[1,64,16,2,256]{4,3,2,1,0:T(2,128)(2,1)S(1)} %bitcast.14) | data formatting | bytes 2097152
  (4 shorter events, 0.1 us)
Async XLA Ops:
  0.0 0.7 %copy-start.5 = (bf16[1,9,64,4]{2,3,1,0:T(4,128)(2,1)S(1)}, bf16[1,9,64,4]{2,3,1,0:T(4,128)(2,1)}, u32[]{:S(2)}) copy-start(bf16[1,9,64,4]{2,3,1,0:T(4,128)(2,1)} %param.8) | copy-start | bytes 13828
  0.0 0.9 %copy-start.4 = (bf16[4,16,2,256]{3,2,1,0:T(2,128)(2,1)S(1)}, bf16[4,16,2,256]{3,2,1,0:T(2,128)(2,1)}, u32[]{:S(2)}) copy-start(bf16[4,16,2,256]{3,2,1,0:T(2,128)(2,1)} %param.6) | copy-start | bytes 196612
  1.0 0.9 %copy-start.1 = (bf16[1,9,64,64]{3,2,1,0:T(8,128)(2,1)S(1)}, bf16[1,9,64,64]{3,2,1,0:T(8,128)(2,1)}, u32[]{:S(2)}) copy-start(bf16[1,9,64,64]{3,2,1,0:T(8,128)(2,1)} %param.10) | copy-start | bytes 221188
  1.0 0.9 %copy-start.2 = (f32[64]{0:T(128)S(1)}, f32[64]{0:T(128)}, u32[]{:S(2)}) copy-start(f32[64]{0:T(128)} %param.9) | copy-start | bytes 772
  1.0 0.9 %copy-start.3 = (f32[64]{0:T(128)S(1)}, f32[64]{0:T(128)}, u32[]{:S(2)}) copy-start(f32[64]{0:T(128)} %param.11) | copy-start | bytes 772
  1.9 1.2 %copy-start = (bf16[1,64,16,2,256]{4,3,2,1,0:T(2,128)(2,1)S(1)}, bf16[1,64,16,2,256]{4,3,2,1,0:T(2,128)(2,1)}, u32[]{:S(2)}) copy-start(bf16[1,64,16,2,256]{4,3,2,1,0:T(2,128)(2,1)} %param.7) | copy-start | bytes 3145732
